TPU v7x, 512 devices: a whole 4x4x16 slice. The times are simulated.
512 devices in a mesh: leaf: 16 (over z), panel: 32 (over y, x, core).
Axes of the slice: x: 4, y: 4, z: 16, core: 2. Of those that a mesh axis runs over, the one named last changes fastest.
Arguments:
- probe_low: bfloat16 [16, 4096, 256], P('leaf', 'panel'), may hold values from -6 to 6
- probe_mid: bfloat16 [16, 2048, 256], P('leaf', 'panel'), may hold values from -6 to 6
- probe_top: bfloat16 [16, 1024, 256], P('leaf', 'panel'), may hold values from -6 to 6
- inv_low: bfloat16 [16, 4096, 4096], P('leaf', 'panel'), may hold values from -0.09375 to 0.09375
- inv_mid: bfloat16 [16, 2048, 4096], P('leaf', 'panel'), may hold values from -0.09375 to 0.09375
- inv_top: bfloat16 [16, 1024, 4096], P('leaf', 'panel'), may hold values from -0.09375 to 0.09375
- gram_low: bfloat16 [16, 4096, 4096], P('leaf', 'panel'), may hold values from -0.09375 to 0.09375
- gram_mid: bfloat16 [16, 2048, 4096], P('leaf', 'panel'), may hold values from -0.09375 to 0.09375
- gram_top: bfloat16 [16, 1024, 4096], P('leaf', 'panel'), may hold values from -0.09375 to 0.09375
- panel_low: bfloat16 [16, 1024, 4096], P('leaf', 'panel'), may hold values from -0.09375 to 0.09375
- panel_mid: bfloat16 [16, 512, 4096], P('leaf', 'panel'), may hold values from -0.09375 to 0.09375
- back_low: bfloat16 [16, 4096, 1024], P('leaf', 'panel'), may hold values from -0.1875 to 0.1875
- back_mid: bfloat16 [16, 2048, 1024], P('leaf', 'panel'), may hold values from -0.1875 to 0.1875
- sep_low: int32 [16, 1024], replicated, may hold values from 0 to 4095, as said below
- sep_mid: int32 [8, 1024], replicated, may hold values from 0 to 4095, as said below
Outputs:
- half_low: bfloat16 [16, 4096, 256], P('leaf', 'panel')
- half_mid: bfloat16 [16, 2048, 256], P('leaf', 'panel')
- half_top: bfloat16 [16, 1024, 256], P('leaf', 'panel')
- solved_low: bfloat16 [16, 4096, 256], P('leaf', 'panel')
- solved_mid: bfloat16 [16, 2048, 256], P('leaf', 'panel')
- solved_top: bfloat16 [16, 1024, 256], P('leaf', 'panel')
Inputs may be any that keep to these rules, and one draw needn't show every extreme that they name: Each row of sep_low lists 1024 distinct rows of a parent supernode; 0 and 4095 occur in every row. Each row of sep_mid lists 1024 distinct rows of a parent supernode; 0 and 4095 occur in every row.
All inputs are finite; a program needn't handle non-finite values.
Results may differ from a plain program's by a relative error of at most 0.0085.
Values may be sent and summed in bfloat16 or wider, within the bound.
A program may use at most 64 MiB of HBM per device.

v0:
```python
import jax
import jax.numpy as jnp
from jax import lax
from jax.sharding import PartitionSpec as P


def from_partner(value, axis, bit):
    mask = 2**bit
    pairs = [(source, source ^ mask) for source in range(lax.axis_size(axis))]
    return lax.ppermute(value, axis, pairs)


def pair_up(block, bit):
    partner = from_partner(block, "leaf", bit)
    upper = lax.axis_index("leaf") >> bit & 1 == 1
    return jnp.where(
        upper, jnp.concatenate([partner, block], 0), jnp.concatenate([block, partner], 0)
    )


def sibling(block, bit):
    return from_partner(block, "leaf", bit)


def collect(piece, depth):
    whole = lax.all_gather(piece, "panel", axis=1, tiled=True)
    for bit in range(depth):
        whole = pair_up(whole, bit)
    return whole.reshape(-1, whole.shape[-1])


def product(matrix, rhs):
    return jnp.dot(matrix[0], rhs, preferred_element_type=jnp.float32)


def own_rows(full, depth, count):
    block = lax.axis_index("leaf") & (1 << depth) - 1
    start = (block * lax.axis_size("panel") + lax.axis_index("panel")) * count
    return lax.dynamic_slice_in_dim(full, start, count, 0)


def child_total(updates, other, rows_table, depth, height):
    child = lax.axis_index("leaf") >> depth
    own_map = lax.dynamic_index_in_dim(rows_table, child, 0, keepdims=False)
    other_map = lax.dynamic_index_in_dim(rows_table, child ^ 1, 0, keepdims=False)
    total = jnp.zeros((height, updates.shape[1]), jnp.float32)
    total = total.at[own_map].add(updates.astype(jnp.float32))
    return total.at[other_map].add(other.astype(jnp.float32))


def parent_side(updates, other, rows_table, depth, probe_local):
    count = probe_local.shape[1]
    total = child_total(
        updates, other, rows_table, depth, count * lax.axis_size("panel") * (2 << depth)
    )
    local = probe_local[0].astype(jnp.float32) - own_rows(total, depth + 1, count)
    return local.astype(jnp.bfloat16)[None]


def sweeps(
    probe_low,
    probe_mid,
    probe_top,
    inv_low,
    inv_mid,
    inv_top,
    gram_low,
    gram_mid,
    gram_top,
    panel_low,
    panel_mid,
    back_low,
    back_mid,
    sep_low,
    sep_mid,
):
    leaf_index = lax.axis_index("leaf")
    right_low = collect(probe_low, 0)
    update_low = product(panel_low, right_low).astype(jnp.bfloat16)
    update_low = collect(update_low[None], 0)
    right_mid = collect(parent_side(update_low, sibling(update_low, 0), sep_low, 0, probe_mid), 1)
    update_mid = product(panel_mid, right_mid).astype(jnp.bfloat16)
    update_mid = collect(update_mid[None], 1)
    right_top = collect(parent_side(update_mid, sibling(update_mid, 1), sep_mid, 1, probe_top), 2)
    half_low = product(inv_low, right_low).astype(jnp.bfloat16)
    half_mid = product(inv_mid, right_mid).astype(jnp.bfloat16)
    half_top = product(inv_top, right_top).astype(jnp.bfloat16)
    solved_top = product(gram_top, right_top).astype(jnp.bfloat16)
    parent_top = collect(solved_top[None], 2)
    map_mid = lax.dynamic_index_in_dim(sep_mid, leaf_index >> 1, 0, keepdims=False)
    taken_mid = jnp.take(parent_top, map_mid, axis=0)
    solved_mid = (product(gram_mid, right_mid) - product(back_mid, taken_mid)).astype(jnp.bfloat16)
    parent_mid = collect(solved_mid[None], 1)
    map_low = lax.dynamic_index_in_dim(sep_low, leaf_index, 0, keepdims=False)
    taken_low = jnp.take(parent_mid, map_low, axis=0)
    solved_low = (product(gram_low, right_low) - product(back_low, taken_low)).astype(jnp.bfloat16)
    return (
        half_low[None],
        half_mid[None],
        half_top[None],
        solved_low[None],
        solved_mid[None],
        solved_top[None],
    )


def body(
    probe_low,
    probe_mid,
    probe_top,
    inv_low,
    inv_mid,
    inv_top,
    gram_low,
    gram_mid,
    gram_top,
    panel_low,
    panel_mid,
    back_low,
    back_mid,
    sep_low,
    sep_mid,
):
    blocks_rest = (
        inv_low,
        inv_mid,
        inv_top,
        gram_low,
        gram_mid,
        gram_top,
        panel_low,
        panel_mid,
        back_low,
        back_mid,
        sep_low,
        sep_mid,
    )
    return sweeps(probe_low, probe_mid, probe_top, *blocks_rest)


def solution(mesh):
    return jax.shard_map(
        body,
        mesh=mesh,
        in_specs=(
            P("leaf", "panel", None),
            P("leaf", "panel", None),
            P("leaf", "panel", None),
            P("leaf", "panel", None),
            P("leaf", "panel", None),
            P("leaf", "panel", None),
            P("leaf", "panel", None),
            P("leaf", "panel", None),
            P("leaf", "panel", None),
            P("leaf", "panel", None),
            P("leaf", "panel", None),
            P("leaf", "panel", None),
            P("leaf", "panel", None),
            P(),
            P(),
        ),
        out_specs=(
            P("leaf", "panel", None),
            P("leaf", "panel", None),
            P("leaf", "panel", None),
            P("leaf", "panel", None),
            P("leaf", "panel", None),
            P("leaf", "panel", None),
        ),
        check_vma=False,
    )
```

profile of v0, /device:TPU:1, one launch (start us, length us, event | category | flops | bytes accessed | tf_op | source)
XLA Modules:
  0.0 584.4 jit_solution(5055272088833783193)
XLA Ops:
  8.0 68.1 %all-gather.10.cloned.1.call-done = bf16[1,4096,256]{2,1,0:T(8,128)(2,1)} async-done(((bf16[1,128,256]{2,1,0:T(8,128)(2,1)}), bf16[1,4096,256]{2,1,0:T(8,128)(2,1)}) %all-gather.10.cloned.1.call-update) | async-done | bytes 2097168 | tf_op jit(solution)/shard_map/all_gather | solution.py:26
  78.2 24.0 %all-gather = bf16[1024,256]{1,0:T(8,128)(2,1)S(1)} all-gather(bf16[32,256]{1,0:T(8,128)(2,1)S(1)} %fusion.21), channel_id=2, replica_groups=mesh['leaf'=16,'panel'=32] {'panel'}, dimensions={0}, use_global_device_ids=true | all-gather | bytes 540672 | tf_op jit(solution)/shard_map/all_gather | solution.py:26
  106.3 8.3 %scatter_custom_fusion = f32[4096,256]{1,0:T(8,128)} fusion(s32[1024]{0:T(1024)S(1)} %bitcast.132, f32[]{:T(128)} %constant.45.clone.1, bf16[1024,256]{1,0:T(8,128)(2,1)S(1)} %all-gather), kind=kCustom, calls=%fused_computation.18 | custom fusion | flops 524288 | bytes 4718596 | tf_op jit(solution)/shard_map/scatter-add | solution.py:47
  117.5 10.2 %scatter_custom_fusion.1 = f32[4096,256]{1,0:T(8,128)} fusion(f32[4096,256]{1,0:T(8,128)} %scatter_custom_fusion, s32[1024]{0:T(1024)S(1)} %bitcast.131, bf16[1024,256]{1,0:T(8,128)(2,1)S(1)} %collective-permute-done), kind=kCustom, calls=%fused_computation.43 | custom fusion | flops 524288 | bytes 4718592 | tf_op jit(solution)/shard_map/scatter-add | solution.py:48
  129.2 57.7 %all-gather.12.cloned.1.call-done = bf16[2048,256]{1,0:T(8,128)(2,1)} async-done(((bf16[64,256]{1,0:T(8,128)(2,1)}), bf16[2048,256]{1,0:T(8,128)(2,1)}) %all-gather.12.cloned.1.call-update) | async-done | bytes 1048592 | tf_op jit(solution)/shard_map/all_gather | solution.py:26
  190.1 23.5 %collective-permute-done.1 = bf16[1,2048,256]{2,1,0:T(8,128)(2,1)} collective-permute-done((bf16[1,2048,256]{2,1,0:T(8,128)(2,1)}, bf16[1,2048,256]{2,1,0:T(8,128)(2,1)}, u32[]{:S(2)}, u32[]{:S(2)}) %collective-permute-start.1) | collective-permute-done | bytes 1048608 | tf_op jit(solution)/shard_map/ppermute | solution.py:10
  216.6 24.9 %all-gather.2 = bf16[512,256]{1,0:T(8,128)(2,1)S(1)} all-gather(bf16[16,256]{1,0:T(8,128)(2,1)S(1)} %fusion.25), channel_id=4, replica_groups=mesh['leaf'=16,'panel'=32] {'panel'}, dimensions={0}, use_global_device_ids=true | all-gather | bytes 270336 | tf_op jit(solution)/shard_map/all_gather | solution.py:26
  244.8 6.5 %collective-permute-done.2 = bf16[1,512,256]{2,1,0:T(8,128)(2,1)S(1)} collective-permute-done((bf16[1,512,256]{2,1,0:T(8,128)(2,1)S(1)}, bf16[1,512,256]{2,1,0:T(8,128)(2,1)S(1)}, u32[]{:S(2)}, u32[]{:S(2)}) %collective-permute-start.2) | collective-permute-done | bytes 262176 | tf_op jit(solution)/shard_map/ppermute | solution.py:10
  252.1 4.3 collective-permute-start.3
  257.3 8.1 %scatter_custom_fusion.2 = f32[4096,256]{1,0:T(8,128)} fusion(s32[1024]{0:T(1024)S(1)} %bitcast.134, f32[]{:T(128)} %constant.45.clone.1, bf16[1024,256]{1,0:T(8,128)(2,1)} %bitcast.20), kind=kCustom, calls=%fused_computation.16 | custom fusion | flops 524288 | bytes 4718596 | tf_op jit(solution)/shard_map/scatter-add | solution.py:47
  265.4 13.8 %collective-permute-done.3 = bf16[1024,256]{1,0:T(8,128)(2,1)} collective-permute-done((bf16[1024,256]{1,0:T(8,128)(2,1)}, bf16[1024,256]{1,0:T(8,128)(2,1)}, u32[]{:S(2)}, u32[]{:S(2)}) %collective-permute-start.3) | collective-permute-done | bytes 524320 | tf_op jit(solution)/shard_map/ppermute | solution.py:10
  279.2 10.6 %scatter_custom_fusion.3 = f32[4096,256]{1,0:T(8,128)} fusion(f32[4096,256]{1,0:T(8,128)} %scatter_custom_fusion.2, s32[1024]{0:T(1024)S(1)} %bitcast.133, bf16[1024,256]{1,0:T(8,128)(2,1)} %collective-permute-done.3), kind=kCustom, calls=%fused_computation.40 | custom fusion | flops 524288 | bytes 4718592 | tf_op jit(solution)/shard_map/scatter-add | solution.py:48
  290.6 24.0 %all-gather.3 = bf16[1024,256]{1,0:T(8,128)(2,1)S(1)} all-gather(bf16[32,256]{1,0:T(8,128)(2,1)S(1)} %fusion.50), channel_id=5, replica_groups=mesh['leaf'=16,'panel'=32] {'panel'}, dimensions={0}, use_global_device_ids=true | all-gather | bytes 540672 | tf_op jit(solution)/shard_map/all_gather | solution.py:26
  316.8 13.0 %collective-permute-done.4 = bf16[1,1024,256]{2,1,0:T(8,128)(2,1)S(1)} collective-permute-done((bf16[1,1024,256]{2,1,0:T(8,128)(2,1)S(1)}, bf16[1,1024,256]{2,1,0:T(8,128)(2,1)S(1)}, u32[]{:S(2)}, u32[]{:S(2)}) %collective-permute-start.4) | collective-permute-done | bytes 524320 | tf_op jit(solution)/shard_map/ppermute | solution.py:10
  330.9 4.1 collective-permute-start.5
  335.1 45.6 %collective-permute-done.5 = bf16[2,1024,256]{2,1,0:T(8,128)(2,1)} collective-permute-done((bf16[2,1024,256]{2,1,0:T(8,128)(2,1)}, bf16[2,1024,256]{2,1,0:T(8,128)(2,1)}, u32[]{:S(2)}, u32[]{:S(2)}) %collective-permute-start.5) | collective-permute-done | bytes 1048608 | tf_op jit(solution)/shard_map/ppermute | solution.py:10
  383.8 25.3 %all-gather.4 = bf16[1024,256]{1,0:T(8,128)(2,1)S(1)} all-gather(bf16[32,256]{1,0:T(8,128)(2,1)S(1)} %bitcast.125), channel_id=6, replica_groups=mesh['leaf'=16,'panel'=32] {'panel'}, dimensions={0}, use_global_device_ids=true | all-gather | bytes 540672 | tf_op jit(solution)/shard_map/all_gather | solution.py:26
  411.3 13.1 %collective-permute-done.6 = bf16[1,1024,256]{2,1,0:T(8,128)(2,1)S(1)} collective-permute-done((bf16[1,1024,256]{2,1,0:T(8,128)(2,1)S(1)}, bf16[1,1024,256]{2,1,0:T(8,128)(2,1)S(1)}, u32[]{:S(2)}, u32[]{:S(2)}) %collective-permute-start.6) | collective-permute-done | bytes 524320 | tf_op jit(solution)/shard_map/ppermute | solution.py:10
  424.5 4.1 collective-permute-start.7
  428.6 45.4 %collective-permute-done.7 = bf16[2,1024,256]{2,1,0:T(8,128)(2,1)S(1)} collective-permute-done((bf16[2,1024,256]{2,1,0:T(8,128)(2,1)S(1)}, bf16[2,1024,256]{2,1,0:T(8,128)(2,1)S(1)}, u32[]{:S(2)}, u32[]{:S(2)}) %collective-permute-start.7) | collective-permute-done | bytes 1048608 | tf_op jit(solution)/shard_map/ppermute | solution.py:10
  475.7 6.5 %gather_fusion = bf16[1024,256]{1,0:T(8,128)(2,1)} fusion(bf16[4096,256]{1,0:T(8,128)(2,1)} %bitcast.111, s32[1024]{0:T(1024)S(1)} %fusion.51), kind=kCustom, calls=%fused_computation.clone | custom fusion | bytes 1052672 | tf_op jit(solution)/shard_map/jit(_take)/gather | solution.py:91
  486.5 57.2 %all-gather.14.cloned.1.call-done = bf16[2048,256]{1,0:T(8,128)(2,1)} async-done(((bf16[64,256]{1,0:T(8,128)(2,1)}), bf16[2048,256]{1,0:T(8,128)(2,1)}) %all-gather.14.cloned.1.call-update) | async-done | bytes 1048592 | tf_op jit(solution)/shard_map/all_gather | solution.py:26
  553.5 17.0 %collective-permute-done.8 = bf16[1,2048,256]{2,1,0:T(8,128)(2,1)S(1)} collective-permute-done((bf16[1,2048,256]{2,1,0:T(8,128)(2,1)}, bf16[1,2048,256]{2,1,0:T(8,128)(2,1)S(1)}, u32[]{:S(2)}, u32[]{:S(2)}) %collective-permute-start.8) | collective-permute-done | bytes 1048608 | tf_op jit(solution)/shard_map/ppermute | solution.py:10
  570.9 4.9 gather_fusion.1
  (69 shorter events, 50.3 us)
Async XLA Ops:
  7.2 539.9 %copy-start = (bf16[1,128,4096]{2,1,0:T(8,128)(2,1)S(1)}, bf16[1,128,4096]{2,1,0:T(8,128)(2,1)}, u32[]{:S(2)}) copy-start(bf16[1,128,4096]{2,1,0:T(8,128)(2,1)} %param.20) | copy-start | bytes 3145732
  7.2 68.9 %all-gather.10.cloned.1.call-start = ((), (), s32[]{:S(2)}) async-start(), calls=%async_computation | async-start | bytes 2162688 | tf_op jit(solution)/shard_map/all_gather | solution.py:26
  7.9 179.0 %all-gather.12.cloned.1.call-start = ((), (), s32[]{:S(2)}) async-start(), calls=%async_computation.1 | async-start | bytes 1081344 | tf_op jit(solution)/shard_map/all_gather | solution.py:26
  102.2 15.3 %collective-permute-start = (bf16[1024,256]{1,0:T(8,128)(2,1)S(1)}, bf16[1024,256]{1,0:T(8,128)(2,1)S(1)}, u32[]{:S(2)}, u32[]{:S(2)}) collective-permute-start(bf16[1024,256]{1,0:T(8,128)(2,1)S(1)} %all-gather), channel_id=1, source_target_pairs={{0,32},{32,0},{64,96},{96,64},{128,160},{160,128},{192,224},{224,1... | collective-permute-start | bytes 1572872 | tf_op jit(solution)/shard_map/ppermute | solution.py:10
  117.5 10.2 %copy-start.11 = (bf16[1,64,256]{2,1,0:T(8,128)(2,1)S(1)}, bf16[1,64,256]{2,1,0:T(8,128)(2,1)}, u32[]{:S(2)}) copy-start(bf16[1,64,256]{2,1,0:T(8,128)(2,1)} %param.18) | copy-start | bytes 98308
  129.2 414.4 %all-gather.14.cloned.1.call-start = ((), (), s32[]{:S(2)}) async-start(), calls=%async_computation.2 | async-start | bytes 1081344 | tf_op jit(solution)/shard_map/all_gather | solution.py:26
  186.9 26.7 %collective-permute-start.1 = (bf16[1,2048,256]{2,1,0:T(8,128)(2,1)}, bf16[1,2048,256]{2,1,0:T(8,128)(2,1)}, u32[]{:S(2)}, u32[]{:S(2)}) collective-permute-start(bf16[1,2048,256]{2,1,0:T(8,128)(2,1)} %bitcast.119), channel_id=1, source_target_pairs={{0,32},{32,0},{64,96},{96,64},{128,160},{160,128},{192,224},{224,1... | collective-permute-start | bytes 3145736 | tf_op jit(solution)/shard_map/ppermute | solution.py:10
  190.1 26.2 %copy-start.9 = (bf16[1,16,4096]{2,1,0:T(8,128)(2,1)S(1)}, bf16[1,16,4096]{2,1,0:T(8,128)(2,1)}, u32[]{:S(2)}) copy-start(bf16[1,16,4096]{2,1,0:T(8,128)(2,1)} %param.27) | copy-start | bytes 393220
  241.6 9.6 %collective-permute-start.2 = (bf16[1,512,256]{2,1,0:T(8,128)(2,1)S(1)}, bf16[1,512,256]{2,1,0:T(8,128)(2,1)S(1)}, u32[]{:S(2)}, u32[]{:S(2)}) collective-permute-start(bf16[1,512,256]{2,1,0:T(8,128)(2,1)S(1)} %bitcast.121), channel_id=1, source_target_pairs={{0,32},{32,0},{64,96},{96,64},{128,160},{160,128},{192,224},{224,1... | collective-permute-start | bytes 786440 | tf_op jit(solution)/shard_map/ppermute | solution.py:10
  252.1 27.1 %collective-permute-start.3 = (bf16[1024,256]{1,0:T(8,128)(2,1)}, bf16[1024,256]{1,0:T(8,128)(2,1)}, u32[]{:S(2)}, u32[]{:S(2)}) collective-permute-start(bf16[1024,256]{1,0:T(8,128)(2,1)} %bitcast.20), channel_id=1, source_target_pairs={{0,64},{32,96},{64,0},{96,32},{128,192},{160,224},{192,128},{224,1... | collective-permute-start | bytes 1572872 | tf_op jit(solution)/shard_map/ppermute | solution.py:10
  279.2 10.6 %copy-start.12 = (bf16[1,32,256]{2,1,0:T(8,128)(2,1)S(1)}, bf16[1,32,256]{2,1,0:T(8,128)(2,1)}, u32[]{:S(2)}) copy-start(bf16[1,32,256]{2,1,0:T(8,128)(2,1)} %param.19) | copy-start | bytes 49156
  314.5 15.3 %collective-permute-start.4 = (bf16[1,1024,256]{2,1,0:T(8,128)(2,1)S(1)}, bf16[1,1024,256]{2,1,0:T(8,128)(2,1)S(1)}, u32[]{:S(2)}, u32[]{:S(2)}) collective-permute-start(bf16[1,1024,256]{2,1,0:T(8,128)(2,1)S(1)} %bitcast.113), channel_id=1, source_target_pairs={{0,32},{32,0},{64,96},{96,64},{128,160},{160,128},{192,224},{224,1... | collective-permute-start | bytes 1572872 | tf_op jit(solution)/shard_map/ppermute | solution.py:10
  330.9 49.8 %collective-permute-start.5 = (bf16[2,1024,256]{2,1,0:T(8,128)(2,1)}, bf16[2,1024,256]{2,1,0:T(8,128)(2,1)}, u32[]{:S(2)}, u32[]{:S(2)}) collective-permute-start(bf16[2,1024,256]{2,1,0:T(8,128)(2,1)} %maximum_select_fusion.4), channel_id=1, source_target_pairs={{0,64},{32,96},{64,0},{96,32},{128,192},{160,224},{192,128},{224,1... | collective-permute-start | bytes 3145736 | tf_op jit(solution)/shard_map/ppermute | solution.py:10
  335.1 48.3 %copy-start.7 = (bf16[1,32,4096]{2,1,0:T(8,128)(2,1)S(1)}, bf16[1,32,4096]{2,1,0:T(8,128)(2,1)}, u32[]{:S(2)}) copy-start(bf16[1,32,4096]{2,1,0:T(8,128)(2,1)} %param.25) | copy-start | bytes 786436
  383.3 41.2 %copy-start.2 = (bf16[4,1024,256]{2,1,0:T(8,128)(2,1)}, bf16[4,1024,256]{2,1,0:T(8,128)(2,1)S(1)}, u32[]{:S(2)}) copy-start(bf16[4,1024,256]{2,1,0:T(8,128)(2,1)S(1)} %maximum_select_fusion.1) | copy-start | bytes 6291460
  383.8 91.9 %copy-start.10 = (bf16[256,32]{0,1:T(8,128)(2,1)}, bf16[256,32]{0,1:T(8,128)(2,1)S(1)}, u32[]{:S(2)}) copy-start(bf16[256,32]{0,1:T(8,128)(2,1)S(1)} %convolution_convert_fusion.1) | copy-start | bytes 49156
  409.1 15.3 %collective-permute-start.6 = (bf16[1,1024,256]{2,1,0:T(8,128)(2,1)S(1)}, bf16[1,1024,256]{2,1,0:T(8,128)(2,1)S(1)}, u32[]{:S(2)}, u32[]{:S(2)}) collective-permute-start(bf16[1,1024,256]{2,1,0:T(8,128)(2,1)S(1)} %bitcast.115), channel_id=1, source_target_pairs={{0,32},{32,0},{64,96},{96,64},{128,160},{160,128},{192,224},{224,1... | collective-permute-start | bytes 1572872 | tf_op jit(solution)/shard_map/ppermute | solution.py:10
  424.5 49.5 %collective-permute-start.7 = (bf16[2,1024,256]{2,1,0:T(8,128)(2,1)S(1)}, bf16[2,1024,256]{2,1,0:T(8,128)(2,1)S(1)}, u32[]{:S(2)}, u32[]{:S(2)}) collective-permute-start(bf16[2,1024,256]{2,1,0:T(8,128)(2,1)S(1)} %maximum_select_fusion.5), channel_id=1, source_target_pairs={{0,64},{32,96},{64,0},{96,32},{128,192},{160,224},{192,128},{224,1... | collective-permute-start | bytes 3145736 | tf_op jit(solution)/shard_map/ppermute | solution.py:10
  475.7 6.5 %copy-start.14 = (bf16[1,64,1024]{2,1,0:T(8,128)(2,1)S(1)}, bf16[1,64,1024]{2,1,0:T(8,128)(2,1)}, u32[]{:S(2)}) copy-start(bf16[1,64,1024]{2,1,0:T(8,128)(2,1)} %param.29) | copy-start | bytes 393220
  543.6 6.1 %copy-start.1 = (bf16[1,4096,256]{2,1,0:T(8,128)(2,1)S(1)}, bf16[1,4096,256]{2,1,0:T(8,128)(2,1)}, u32[]{:S(2)}) copy-start(bf16[1,4096,256]{2,1,0:T(8,128)(2,1)} %all-gather.10.cloned.1.call-done) | copy-start | bytes 6291460
  543.6 6.1 %copy-start.4 = (bf16[1,128,4096]{2,1,0:T(8,128)(2,1)S(1)}, bf16[1,128,4096]{2,1,0:T(8,128)(2,1)}, u32[]{:S(2)}) copy-start(bf16[1,128,4096]{2,1,0:T(8,128)(2,1)} %param.23) | copy-start | bytes 3145732
  543.6 26.9 %collective-permute-start.8 = (bf16[1,2048,256]{2,1,0:T(8,128)(2,1)}, bf16[1,2048,256]{2,1,0:T(8,128)(2,1)S(1)}, u32[]{:S(2)}, u32[]{:S(2)}) collective-permute-start(bf16[1,2048,256]{2,1,0:T(8,128)(2,1)} %bitcast.117), channel_id=1, source_target_pairs={{0,32},{32,0},{64,96},{96,64},{128,160},{160,128},{192,224},{224,1... | collective-permute-start | bytes 3145736 | tf_op jit(solution)/shard_map/ppermute | solution.py:10
  550.8 19.7 %copy-start.5 = (bf16[2048,256]{1,0:T(8,128)(2,1)S(1)}, bf16[2048,256]{1,0:T(8,128)(2,1)}, u32[]{:S(2)}) copy-start(bf16[2048,256]{1,0:T(8,128)(2,1)} %all-gather.14.cloned.1.call-done) | copy-start | bytes 3145732
  570.9 5.0 copy-start.13
  (3 other events, 4.8 us)
Sparse Core Ops, SparseCore 0:
  11.2 64.8 all-gather.9
  129.3 57.5 all-gather.11
  485.8 57.7 all-gather.13
where the time goes:
time: 585 us; the launch traced here: 584 us
  waiting for transfers between devices  364 us (62%)
  blocking collectives  98.2 us (17%)
  other arithmetic  50.5 us (9%)
  starting transfers between devices  30.1 us (5%)
  between operations  14 us (2%)
  matrix products  13.8 us (2%)
  local copies, waits for them, and re-layouts  13.4 us (2%)
    all_gather x3, waiting for transfers between devices, collect(): whole = lax.all_gather(piece, 'panel', axis=1, tiled=True)  183 us
    ppermute x9, waiting for transfers between devices, from_partner(): return lax.ppermute(value, axis, pairs)  181 us
    all_gather x4, blocking collectives, collect(): whole = lax.all_gather(piece, 'panel', axis=1, tiled=True)  98.2 us
    ppermute x9, starting transfers between devices, from_partner(): return lax.ppermute(value, axis, pairs)  29.9 us
    scatter-add x2, other arithmetic, child_total(): return total.at[other_map].add(other.astype(jnp.float32))  20.8 us
    scatter-add x2, other arithmetic, child_total(): total = total.at[own_map].add(updates.astype(jnp.float32))  16.4 us
    dot_general x10, matrix products, product(): return jnp.dot(matrix[0], rhs, preferred_element_type=jnp.float32)  13.8 us
  transfers between devices with their start and end apart: 12, of which 12 were waited for; matrix products, arithmetic and copies ran while one was open for 4% of the time, Pallas kernels for 0%

commit v1 on v0

--- a/solution.py
+++ b/solution.py
@@ -2,6 +2,28 @@
 import jax.numpy as jnp
 from jax import lax
 from jax.sharding import PartitionSpec as P
+
+
+def laid_out(blocks, dim):
+    lengths = list(blocks.shape[1:])
+    lengths[dim] *= blocks.shape[0]
+    return jnp.moveaxis(blocks, 0, dim).reshape(lengths)
+
+
+def collected_by_bits(x, axis):
+    devices = lax.axis_size(axis)
+    tiles = x[None]
+    for level in range(devices.bit_length() - 1):
+        stride = 1 << level
+        other = lax.ppermute(tiles, axis, [(i, i ^ stride) for i in range(devices)])
+        both = jnp.stack([tiles, other])
+        upper = lax.axis_index(axis) >> level & 1
+        tiles = jnp.where(upper == 0, both, both[::-1]).reshape(-1, *x.shape)
+    return tiles
+
+
+def gather_by_bits(shard, axis, dim):
+    return laid_out(collected_by_bits(shard, axis), dim)
 
 
 def from_partner(value, axis, bit):
@@ -23,7 +45,7 @@
 
 
 def collect(piece, depth):
-    whole = lax.all_gather(piece, "panel", axis=1, tiled=True)
+    whole = gather_by_bits(piece, "panel", 1)
     for bit in range(depth):
         whole = pair_up(whole, bit)
     return whole.reshape(-1, whole.shape[-1])

time: 585 us -> 550 us (0.940)
  starting transfers between devices: 30.1 us -> 129 us
  blocking collectives: 98.2 us -> 0 us
  waiting for transfers between devices: 364 us -> 320 us
  other arithmetic: 50.5 us -> 63.5 us
  between operations: 14 us -> 1.58 us
    all_gather x3 -> x0, waiting for transfers between devices: 183 us -> none  [collect(): whole = lax.all_gather(piece, 'panel', axis=1, tiled=True)]
    ppermute x0 -> x35, waiting for transfers between devices: none -> 153 us  [collected_by_bits(): other = lax.ppermute(tiles, axis, [(i, i ^ stride) for i in range(devices)])]
    ppermute x0 -> x35, starting transfers between devices: none -> 110 us  [collected_by_bits(): other = lax.ppermute(tiles, axis, [(i, i ^ stride) for i in range(devices)])]
    all_gather x4 -> x0, blocking collectives: 98.2 us -> none  [collect(): whole = lax.all_gather(piece, 'panel', axis=1, tiled=True)]
    ppermute x9, waiting for transfers between devices: 181 us -> 168 us  [from_partner(): return lax.ppermute(value, axis, pairs)]
    ppermute x9, starting transfers between devices: 29.9 us -> 19.8 us  [from_partner(): return lax.ppermute(value, axis, pairs)]
    select_n x0 -> x28, other arithmetic: none -> 6.04 us  [collected_by_bits(): tiles = jnp.where(upper == 0, both, both[::-1]).reshape(-1, *x.shape)]
  transfers between devices with their start and end apart: 12 -> 44, of which waited for: 12 -> 43; matrix products, arithmetic and copies ran while one was open for 4% -> 4% of each run, Pallas kernels for 0% -> 0%
where the time goes in v1:
time: 550 us; the launch traced here: 544 us
  waiting for transfers between devices  320 us (58%)
  starting transfers between devices  129 us (23%)
  other arithmetic  63.5 us (12%)
  local copies, waits for them, and re-layouts  15.7 us (3%)
  matrix products  13.3 us (2%)
    ppermute x9, waiting for transfers between devices, from_partner(): return lax.ppermute(value, axis, pairs)  168 us
    ppermute x35, waiting for transfers between devices, collected_by_bits(): other = lax.ppermute(tiles, axis, [(i, i ^ stride) for i in range(devices)])  153 us
    ppermute x35, starting transfers between devices, collected_by_bits(): other = lax.ppermute(tiles, axis, [(i, i ^ stride) for i in range(devices)])  110 us
    scatter-add x2, other arithmetic, child_total(): return total.at[other_map].add(other.astype(jnp.float32))  21.3 us
    ppermute x9, starting transfers between devices, from_partner(): return lax.ppermute(value, axis, pairs)  19.8 us
    scatter-add x2, other arithmetic, child_total(): total = total.at[own_map].add(updates.astype(jnp.float32))  16.4 us
    dot_general x10, matrix products, product(): return jnp.dot(matrix[0], rhs, preferred_element_type=jnp.float32)  13.3 us
    select_n x7, other arithmetic, pair_up(): jnp.where(upper, jnp.concatenate([partner, block], 0), jnp.concatenate([b...  13.2 us
  transfers between devices with their start and end apart: 44, of which 43 were waited for; matrix products, arithmetic and copies ran while one was open for 4% of the time, Pallas kernels for 0%

profile of v1, /device:TPU:1, one launch (start us, length us, event | category | flops | bytes accessed | tf_op | source)
XLA Modules:
  0.0 543.7 jit_solution(782943793851688948)
XLA Ops:
  0.6 8.9 %collective-permute-start = (bf16[1,1,128,256]{3,2,1,0:T(8,128)(2,1)}, bf16[1,1,128,256]{3,2,1,0:T(8,128)(2,1)S(1)}, u32[]{:S(2)}, u32[]{:S(2)}) collective-permute-start(bf16[1,1,128,256]{3,2,1,0:T(8,128)(2,1)} %bitcast.325), channel_id=1, source_target_pairs={{0,1},{1,0},{2,3},{3,2},{4,5},{5,4},{6,7},{7,6},{8,9},{9,8},{10,11... | collective-permute-start | bytes 196616 | tf_op jit(solution)/shard_map/ppermute | solution.py:18
  20.2 8.1 %collective-permute-done.2 = bf16[4,1,128,256]{3,2,0,1:T(8,128)(2,1)S(1)} collective-permute-done((bf16[4,1,128,256]{3,2,0,1:T(8,128)(2,1)S(1)}, bf16[4,1,128,256]{3,2,0,1:T(8,128)(2,1)S(1)}, u32[]{:S(2)}, u32[]{:S(2)}) %collective-permute-start.2) | collective-permute-done | bytes 262176 | tf_op jit(solution)/shard_map/ppermute | solution.py:18
  30.4 11.3 %collective-permute-done.3 = bf16[8,1,128,256]{3,2,0,1:T(8,128)(2,1)S(1)} collective-permute-done((bf16[8,1,128,256]{3,2,0,1:T(8,128)(2,1)S(1)}, bf16[8,1,128,256]{3,2,0,1:T(8,128)(2,1)S(1)}, u32[]{:S(2)}, u32[]{:S(2)}) %collective-permute-start.3) | collective-permute-done | bytes 524320 | tf_op jit(solution)/shard_map/ppermute | solution.py:18
  43.9 23.1 %collective-permute-done.4 = bf16[16,1,128,256]{3,2,0,1:T(8,128)(2,1)S(1)} collective-permute-done((bf16[16,1,128,256]{3,2,0,1:T(8,128)(2,1)S(1)}, bf16[16,1,128,256]{3,2,0,1:T(8,128)(2,1)S(1)}, u32[]{:S(2)}, u32[]{:S(2)}) %collective-permute-start.4) | collective-permute-done | bytes 1048608 | tf_op jit(solution)/shard_map/ppermute | solution.py:18
  94.3 6.7 %collective-permute-done.9 = bf16[16,1,32,256]{3,2,0,1:T(8,128)(2,1)S(1)} collective-permute-done((bf16[16,1,32,256]{3,2,0,1:T(8,128)(2,1)S(1)}, bf16[16,1,32,256]{3,2,0,1:T(8,128)(2,1)S(1)}, u32[]{:S(2)}, u32[]{:S(2)}) %collective-permute-start.9) | collective-permute-done | bytes 262176 | tf_op jit(solution)/shard_map/ppermute | solution.py:18
  104.7 8.2 %scatter_custom_fusion = f32[4096,256]{1,0:T(8,128)} fusion(s32[1024]{0:T(1024)S(1)} %bitcast.354, f32[]{:T(128)} %constant.51.clone.1, bf16[1024,256]{1,0:T(8,128)(2,1)} %bitcast.41), kind=kCustom, calls=%fused_computation.14 | custom fusion | flops 524288 | bytes 4718596 | tf_op jit(solution)/shard_map/scatter-add | solution.py:69
  112.9 10.6 %scatter_custom_fusion.1 = f32[4096,256]{1,0:T(8,128)} fusion(f32[4096,256]{1,0:T(8,128)} %scatter_custom_fusion, s32[1024]{0:T(1024)S(1)} %bitcast.353, bf16[1024,256]{1,0:T(8,128)(2,1)} %collective-permute-done.10), kind=kCustom, calls=%fused_computation.43 | custom fusion | flops 524288 | bytes 4718592 | tf_op jit(solution)/shard_map/scatter-add | solution.py:70
  124.4 7.5 %collective-permute-start.11 = (bf16[1,1,64,256]{3,2,1,0:T(8,128)(2,1)S(1)}, bf16[1,1,64,256]{3,2,1,0:T(8,128)(2,1)S(1)}, u32[]{:S(2)}, u32[]{:S(2)}) collective-permute-start(bf16[1,1,64,256]{3,2,1,0:T(8,128)(2,1)S(1)} %bitcast.318), channel_id=1, source_target_pairs={{0,1},{1,0},{2,3},{3,2},{4,5},{5,4},{6,7},{7,6},{8,9},{9,8},{10,11... | collective-permute-start | bytes 98312 | tf_op jit(solution)/shard_map/ppermute | solution.py:18
  154.3 11.1 %collective-permute-done.15 = bf16[16,1,64,256]{3,2,0,1:T(8,128)(2,1)S(1)} collective-permute-done((bf16[16,1,64,256]{3,2,0,1:T(8,128)(2,1)S(1)}, bf16[16,1,64,256]{3,2,0,1:T(8,128)(2,1)S(1)}, u32[]{:S(2)}, u32[]{:S(2)}) %collective-permute-start.15) | collective-permute-done | bytes 524320 | tf_op jit(solution)/shard_map/ppermute | solution.py:18
  169.8 19.1 %collective-permute-done.16 = bf16[1,2048,256]{2,1,0:T(8,128)(2,1)} collective-permute-done((bf16[1,2048,256]{2,1,0:T(8,128)(2,1)}, bf16[1,2048,256]{2,1,0:T(8,128)(2,1)}, u32[]{:S(2)}, u32[]{:S(2)}) %collective-permute-start.16) | collective-permute-done | bytes 1048608 | tf_op jit(solution)/shard_map/ppermute | solution.py:32
  192.0 7.5 %collective-permute-start.17 = (bf16[1,1,16,256]{3,2,1,0:T(8,128)(2,1)S(1)}, bf16[1,1,16,256]{3,2,1,0:T(8,128)(2,1)S(1)}, u32[]{:S(2)}, u32[]{:S(2)}) collective-permute-start(bf16[1,1,16,256]{3,2,1,0:T(8,128)(2,1)S(1)} %bitcast.340), channel_id=1, source_target_pairs={{0,1},{1,0},{2,3},{3,2},{4,5},{5,4},{6,7},{7,6},{8,9},{9,8},{10,11... | collective-permute-start | bytes 24584 | tf_op jit(solution)/shard_map/ppermute | solution.py:18
  234.4 8.2 %scatter_custom_fusion.2 = f32[4096,256]{1,0:T(8,128)} fusion(s32[1024]{0:T(1024)S(1)} %bitcast.356, f32[]{:T(128)} %constant.51.clone.1, bf16[1024,256]{1,0:T(8,128)(2,1)} %bitcast.86), kind=kCustom, calls=%fused_computation.12 | custom fusion | flops 524288 | bytes 4718596 | tf_op jit(solution)/shard_map/scatter-add | solution.py:69
  242.5 16.1 %collective-permute-done.23 = bf16[1024,256]{1,0:T(8,128)(2,1)} collective-permute-done((bf16[1024,256]{1,0:T(8,128)(2,1)}, bf16[1024,256]{1,0:T(8,128)(2,1)}, u32[]{:S(2)}, u32[]{:S(2)}) %collective-permute-start.23) | collective-permute-done | bytes 524320 | tf_op jit(solution)/shard_map/ppermute | solution.py:32
  258.7 10.6 %scatter_custom_fusion.3 = f32[4096,256]{1,0:T(8,128)} fusion(f32[4096,256]{1,0:T(8,128)} %scatter_custom_fusion.2, s32[1024]{0:T(1024)S(1)} %bitcast.355, bf16[1024,256]{1,0:T(8,128)(2,1)} %collective-permute-done.23), kind=kCustom, calls=%fused_computation.40 | custom fusion | flops 524288 | bytes 4718592 | tf_op jit(solution)/shard_map/scatter-add | solution.py:70
  293.2 6.7 %collective-permute-done.28 = bf16[16,1,32,256]{3,2,0,1:T(8,128)(2,1)S(1)} collective-permute-done((bf16[16,1,32,256]{3,2,0,1:T(8,128)(2,1)S(1)}, bf16[16,1,32,256]{3,2,0,1:T(8,128)(2,1)S(1)}, u32[]{:S(2)}, u32[]{:S(2)}) %collective-permute-start.28) | collective-permute-done | bytes 262176 | tf_op jit(solution)/shard_map/ppermute | solution.py:18
  302.0 8.4 %collective-permute-done.29 = bf16[1,1024,256]{2,1,0:T(8,128)(2,1)S(1)} collective-permute-done((bf16[1,1024,256]{2,1,0:T(8,128)(2,1)S(1)}, bf16[1,1024,256]{2,1,0:T(8,128)(2,1)S(1)}, u32[]{:S(2)}, u32[]{:S(2)}) %collective-permute-start.29) | collective-permute-done | bytes 524320 | tf_op jit(solution)/shard_map/ppermute | solution.py:32
  313.5 48.7 %collective-permute-done.30 = bf16[2,1024,256]{2,1,0:T(8,128)(2,1)} collective-permute-done((bf16[2,1024,256]{2,1,0:T(8,128)(2,1)}, bf16[2,1024,256]{2,1,0:T(8,128)(2,1)}, u32[]{:S(2)}, u32[]{:S(2)}) %collective-permute-start.30) | collective-permute-done | bytes 1048608 | tf_op jit(solution)/shard_map/ppermute | solution.py:32
  387.6 6.7 %collective-permute-done.35 = bf16[16,1,32,256]{3,2,0,1:T(8,128)(2,1)S(1)} collective-permute-done((bf16[16,1,32,256]{3,2,0,1:T(8,128)(2,1)S(1)}, bf16[16,1,32,256]{3,2,0,1:T(8,128)(2,1)S(1)}, u32[]{:S(2)}, u32[]{:S(2)}) %collective-permute-start.35) | collective-permute-done | bytes 262176 | tf_op jit(solution)/shard_map/ppermute | solution.py:18
  396.4 8.4 %collective-permute-done.36 = bf16[1,1024,256]{2,1,0:T(8,128)(2,1)S(1)} collective-permute-done((bf16[1,1024,256]{2,1,0:T(8,128)(2,1)S(1)}, bf16[1,1024,256]{2,1,0:T(8,128)(2,1)S(1)}, u32[]{:S(2)}, u32[]{:S(2)}) %collective-permute-start.36) | collective-permute-done | bytes 524320 | tf_op jit(solution)/shard_map/ppermute | solution.py:32
  407.0 48.4 %collective-permute-done.37 = bf16[2,1024,256]{2,1,0:T(8,128)(2,1)S(1)} collective-permute-done((bf16[2,1024,256]{2,1,0:T(8,128)(2,1)S(1)}, bf16[2,1024,256]{2,1,0:T(8,128)(2,1)S(1)}, u32[]{:S(2)}, u32[]{:S(2)}) %collective-permute-start.37) | collective-permute-done | bytes 1048608 | tf_op jit(solution)/shard_map/ppermute | solution.py:32
  457.1 6.5 %gather_fusion = bf16[1024,256]{1,0:T(8,128)(2,1)} fusion(bf16[4096,256]{1,0:T(8,128)(2,1)} %bitcast.251, s32[1024]{0:T(1024)S(1)} %fusion.50), kind=kCustom, calls=%fused_computation.clone | custom fusion | bytes 1052672 | tf_op jit(solution)/shard_map/jit(_take)/gather | solution.py:113
  493.6 10.6 %collective-permute-done.42 = bf16[16,1,64,256]{3,2,0,1:T(8,128)(2,1)} collective-permute-done((bf16[16,1,64,256]{3,2,0,1:T(8,128)(2,1)}, bf16[16,1,64,256]{3,2,0,1:T(8,128)(2,1)}, u32[]{:S(2)}, u32[]{:S(2)}) %collective-permute-start.42) | collective-permute-done | bytes 524320 | tf_op jit(solution)/shard_map/ppermute | solution.py:18
  514.5 14.4 %collective-permute-done.43 = bf16[1,2048,256]{2,1,0:T(8,128)(2,1)} collective-permute-done((bf16[1,2048,256]{2,1,0:T(8,128)(2,1)}, bf16[1,2048,256]{2,1,0:T(8,128)(2,1)}, u32[]{:S(2)}, u32[]{:S(2)}) %collective-permute-start.43) | collective-permute-done | bytes 1048608 | tf_op jit(solution)/shard_map/ppermute | solution.py:32
  532.9 6.5 %gather_fusion.1 = bf16[1024,256]{1,0:T(8,128)(2,1)} fusion(bf16[4096,256]{1,0:T(8,128)(2,1)} %bitcast.252, s32[1024]{0:T(1024)S(1)} %fusion.51), kind=kCustom, calls=%fused_computation.1.clone | custom fusion | bytes 1052672 | tf_op jit(solution)/shard_map/jit(_take)/gather | solution.py:117
  (196 shorter events, 219.8 us)
Async XLA Ops:
  0.6 10.0 %collective-permute-start = (bf16[1,1,128,256]{3,2,1,0:T(8,128)(2,1)}, bf16[1,1,128,256]{3,2,1,0:T(8,128)(2,1)S(1)}, u32[]{:S(2)}, u32[]{:S(2)}) collective-permute-start(bf16[1,1,128,256]{3,2,1,0:T(8,128)(2,1)} %bitcast.325), channel_id=1, source_target_pairs={{0,1},{1,0},{2,3},{3,2},{4,5},{5,4},{6,7},{7,6},{8,9},{9,8},{10,11... | collective-permute-start | bytes 196616 | tf_op jit(solution)/shard_map/ppermute | solution.py:18
  18.3 10.0 %collective-permute-start.2 = (bf16[4,1,128,256]{3,2,0,1:T(8,128)(2,1)S(1)}, bf16[4,1,128,256]{3,2,0,1:T(8,128)(2,1)S(1)}, u32[]{:S(2)}, u32[]{:S(2)}) collective-permute-start(bf16[4,1,128,256]{3,2,0,1:T(8,128)(2,1)S(1)} %bitcast.263), channel_id=1, source_target_pairs={{0,4},{1,5},{2,6},{3,7},{4,0},{5,1},{6,2},{7,3},{8,12},{9,13},{10,... | collective-permute-start | bytes 786440 | tf_op jit(solution)/shard_map/ppermute | solution.py:18
  28.4 13.2 %collective-permute-start.3 = (bf16[8,1,128,256]{3,2,0,1:T(8,128)(2,1)S(1)}, bf16[8,1,128,256]{3,2,0,1:T(8,128)(2,1)S(1)}, u32[]{:S(2)}, u32[]{:S(2)}) collective-permute-start(bf16[8,1,128,256]{3,2,0,1:T(8,128)(2,1)S(1)} %bitcast.259), channel_id=1, source_target_pairs={{0,8},{1,9},{2,10},{3,11},{4,12},{5,13},{6,14},{7,15},{8,0},{9,1},... | collective-permute-start | bytes 1572872 | tf_op jit(solution)/shard_map/ppermute | solution.py:18
  42.0 25.0 %collective-permute-start.4 = (bf16[16,1,128,256]{3,2,0,1:T(8,128)(2,1)S(1)}, bf16[16,1,128,256]{3,2,0,1:T(8,128)(2,1)S(1)}, u32[]{:S(2)}, u32[]{:S(2)}) collective-permute-start(bf16[16,1,128,256]{3,2,0,1:T(8,128)(2,1)S(1)} %bitcast.253), channel_id=1, source_target_pairs={{0,16},{1,17},{2,18},{3,19},{4,20},{5,21},{6,22},{7,23},{8,24},{9,... | collective-permute-start | bytes 3145736 | tf_op jit(solution)/shard_map/ppermute | solution.py:18
  92.4 8.6 %collective-permute-start.9 = (bf16[16,1,32,256]{3,2,0,1:T(8,128)(2,1)S(1)}, bf16[16,1,32,256]{3,2,0,1:T(8,128)(2,1)S(1)}, u32[]{:S(2)}, u32[]{:S(2)}) collective-permute-start(bf16[16,1,32,256]{3,2,0,1:T(8,128)(2,1)S(1)} %bitcast.267), channel_id=1, source_target_pairs={{0,16},{1,17},{2,18},{3,19},{4,20},{5,21},{6,22},{7,23},{8,24},{9,... | collective-permute-start | bytes 786440 | tf_op jit(solution)/shard_map/ppermute | solution.py:18
  102.0 11.0 %collective-permute-start.10 = (bf16[1024,256]{1,0:T(8,128)(2,1)}, bf16[1024,256]{1,0:T(8,128)(2,1)}, u32[]{:S(2)}, u32[]{:S(2)}) collective-permute-start(bf16[1024,256]{1,0:T(8,128)(2,1)} %bitcast.41), channel_id=1, source_target_pairs={{0,32},{32,0},{64,96},{96,64},{128,160},{160,128},{192,224},{224,1... | collective-permute-start | bytes 1572872 | tf_op jit(solution)/shard_map/ppermute | solution.py:32
  124.4 8.3 %collective-permute-start.11 = (bf16[1,1,64,256]{3,2,1,0:T(8,128)(2,1)S(1)}, bf16[1,1,64,256]{3,2,1,0:T(8,128)(2,1)S(1)}, u32[]{:S(2)}, u32[]{:S(2)}) collective-permute-start(bf16[1,1,64,256]{3,2,1,0:T(8,128)(2,1)S(1)} %bitcast.318), channel_id=1, source_target_pairs={{0,1},{1,0},{2,3},{3,2},{4,5},{5,4},{6,7},{7,6},{8,9},{9,8},{10,11... | collective-permute-start | bytes 98312 | tf_op jit(solution)/shard_map/ppermute | solution.py:18
  137.8 7.2 %collective-permute-start.13 = (bf16[4,1,64,256]{3,2,0,1:T(8,128)(2,1)S(1)}, bf16[4,1,64,256]{3,2,0,1:T(8,128)(2,1)S(1)}, u32[]{:S(2)}, u32[]{:S(2)}) collective-permute-start(bf16[4,1,64,256]{3,2,0,1:T(8,128)(2,1)S(1)} %bitcast.282), channel_id=1, source_target_pairs={{0,4},{1,5},{2,6},{3,7},{4,0},{5,1},{6,2},{7,3},{8,12},{9,13},{10,... | collective-permute-start | bytes 393224 | tf_op jit(solution)/shard_map/ppermute | solution.py:18
  145.1 7.1 %collective-permute-start.14 = (bf16[8,1,64,256]{3,2,0,1:T(8,128)(2,1)S(1)}, bf16[8,1,64,256]{3,2,0,1:T(8,128)(2,1)S(1)}, u32[]{:S(2)}, u32[]{:S(2)}) collective-permute-start(bf16[8,1,64,256]{3,2,0,1:T(8,128)(2,1)S(1)} %bitcast.269), channel_id=1, source_target_pairs={{0,8},{1,9},{2,10},{3,11},{4,12},{5,13},{6,14},{7,15},{8,0},{9,1},... | collective-permute-start | bytes 786440 | tf_op jit(solution)/shard_map/ppermute | solution.py:18
  152.4 13.0 %collective-permute-start.15 = (bf16[16,1,64,256]{3,2,0,1:T(8,128)(2,1)S(1)}, bf16[16,1,64,256]{3,2,0,1:T(8,128)(2,1)S(1)}, u32[]{:S(2)}, u32[]{:S(2)}) collective-permute-start(bf16[16,1,64,256]{3,2,0,1:T(8,128)(2,1)S(1)} %bitcast.261), channel_id=1, source_target_pairs={{0,16},{1,17},{2,18},{3,19},{4,20},{5,21},{6,22},{7,23},{8,24},{9,... | collective-permute-start | bytes 1572872 | tf_op jit(solution)/shard_map/ppermute | solution.py:18
  166.8 22.1 %collective-permute-start.16 = (bf16[1,2048,256]{2,1,0:T(8,128)(2,1)}, bf16[1,2048,256]{2,1,0:T(8,128)(2,1)}, u32[]{:S(2)}, u32[]{:S(2)}) collective-permute-start(bf16[1,2048,256]{2,1,0:T(8,128)(2,1)} %bitcast.60), channel_id=1, source_target_pairs={{0,32},{32,0},{64,96},{96,64},{128,160},{160,128},{192,224},{224,1... | collective-permute-start | bytes 3145736 | tf_op jit(solution)/shard_map/ppermute | solution.py:32
  192.0 8.4 %collective-permute-start.17 = (bf16[1,1,16,256]{3,2,1,0:T(8,128)(2,1)S(1)}, bf16[1,1,16,256]{3,2,1,0:T(8,128)(2,1)S(1)}, u32[]{:S(2)}, u32[]{:S(2)}) collective-permute-start(bf16[1,1,16,256]{3,2,1,0:T(8,128)(2,1)S(1)} %bitcast.340), channel_id=1, source_target_pairs={{0,1},{1,0},{2,3},{3,2},{4,5},{5,4},{6,7},{7,6},{8,9},{9,8},{10,11... | collective-permute-start | bytes 24584 | tf_op jit(solution)/shard_map/ppermute | solution.py:18
  216.1 7.2 %collective-permute-start.21 = (bf16[16,1,16,256]{3,2,0,1:T(8,128)(2,1)S(1)}, bf16[16,1,16,256]{3,2,0,1:T(8,128)(2,1)S(1)}, u32[]{:S(2)}, u32[]{:S(2)}) collective-permute-start(bf16[16,1,16,256]{3,2,0,1:T(8,128)(2,1)S(1)} %bitcast.284), channel_id=1, source_target_pairs={{0,16},{1,17},{2,18},{3,19},{4,20},{5,21},{6,22},{7,23},{8,24},{9,... | collective-permute-start | bytes 393224 | tf_op jit(solution)/shard_map/ppermute | solution.py:18
  223.4 7.1 %collective-permute-start.22 = (bf16[1,512,256]{2,1,0:T(8,128)(2,1)S(1)}, bf16[1,512,256]{2,1,0:T(8,128)(2,1)S(1)}, u32[]{:S(2)}, u32[]{:S(2)}) collective-permute-start(bf16[1,512,256]{2,1,0:T(8,128)(2,1)S(1)} %bitcast.271), channel_id=1, source_target_pairs={{0,32},{32,0},{64,96},{96,64},{128,160},{160,128},{192,224},{224,1... | collective-permute-start | bytes 786440 | tf_op jit(solution)/shard_map/ppermute | solution.py:32
  231.4 27.3 %collective-permute-start.23 = (bf16[1024,256]{1,0:T(8,128)(2,1)}, bf16[1024,256]{1,0:T(8,128)(2,1)}, u32[]{:S(2)}, u32[]{:S(2)}) collective-permute-start(bf16[1024,256]{1,0:T(8,128)(2,1)} %bitcast.86), channel_id=1, source_target_pairs={{0,64},{32,96},{64,0},{96,32},{128,192},{160,224},{192,128},{224,1... | collective-permute-start | bytes 1572872 | tf_op jit(solution)/shard_map/ppermute | solution.py:32
  291.3 8.6 %collective-permute-start.28 = (bf16[16,1,32,256]{3,2,0,1:T(8,128)(2,1)S(1)}, bf16[16,1,32,256]{3,2,0,1:T(8,128)(2,1)S(1)}, u32[]{:S(2)}, u32[]{:S(2)}) collective-permute-start(bf16[16,1,32,256]{3,2,0,1:T(8,128)(2,1)S(1)} %bitcast.273), channel_id=1, source_target_pairs={{0,16},{1,17},{2,18},{3,19},{4,20},{5,21},{6,22},{7,23},{8,24},{9,... | collective-permute-start | bytes 786440 | tf_op jit(solution)/shard_map/ppermute | solution.py:18
  300.1 10.4 %collective-permute-start.29 = (bf16[1,1024,256]{2,1,0:T(8,128)(2,1)S(1)}, bf16[1,1024,256]{2,1,0:T(8,128)(2,1)S(1)}, u32[]{:S(2)}, u32[]{:S(2)}) collective-permute-start(bf16[1,1024,256]{2,1,0:T(8,128)(2,1)S(1)} %bitcast.255), channel_id=1, source_target_pairs={{0,32},{32,0},{64,96},{96,64},{128,160},{160,128},{192,224},{224,1... | collective-permute-start | bytes 1572872 | tf_op jit(solution)/shard_map/ppermute | solution.py:32
  311.6 50.6 %collective-permute-start.30 = (bf16[2,1024,256]{2,1,0:T(8,128)(2,1)}, bf16[2,1024,256]{2,1,0:T(8,128)(2,1)}, u32[]{:S(2)}, u32[]{:S(2)}) collective-permute-start(bf16[2,1024,256]{2,1,0:T(8,128)(2,1)} %maximum_select_fusion.4), channel_id=1, source_target_pairs={{0,64},{32,96},{64,0},{96,32},{128,192},{160,224},{192,128},{224,1... | collective-permute-start | bytes 3145736 | tf_op jit(solution)/shard_map/ppermute | solution.py:32
  385.7 8.6 %collective-permute-start.35 = (bf16[16,1,32,256]{3,2,0,1:T(8,128)(2,1)S(1)}, bf16[16,1,32,256]{3,2,0,1:T(8,128)(2,1)S(1)}, u32[]{:S(2)}, u32[]{:S(2)}) collective-permute-start(bf16[16,1,32,256]{3,2,0,1:T(8,128)(2,1)S(1)} %bitcast.275), channel_id=1, source_target_pairs={{0,16},{1,17},{2,18},{3,19},{4,20},{5,21},{6,22},{7,23},{8,24},{9,... | collective-permute-start | bytes 786440 | tf_op jit(solution)/shard_map/ppermute | solution.py:18
  394.5 10.4 %collective-permute-start.36 = (bf16[1,1024,256]{2,1,0:T(8,128)(2,1)S(1)}, bf16[1,1024,256]{2,1,0:T(8,128)(2,1)S(1)}, u32[]{:S(2)}, u32[]{:S(2)}) collective-permute-start(bf16[1,1024,256]{2,1,0:T(8,128)(2,1)S(1)} %bitcast.257), channel_id=1, source_target_pairs={{0,32},{32,0},{64,96},{96,64},{128,160},{160,128},{192,224},{224,1... | collective-permute-start | bytes 1572872 | tf_op jit(solution)/shard_map/ppermute | solution.py:32
  405.0 50.3 %collective-permute-start.37 = (bf16[2,1024,256]{2,1,0:T(8,128)(2,1)S(1)}, bf16[2,1024,256]{2,1,0:T(8,128)(2,1)S(1)}, u32[]{:S(2)}, u32[]{:S(2)}) collective-permute-start(bf16[2,1024,256]{2,1,0:T(8,128)(2,1)S(1)} %maximum_select_fusion.5), channel_id=1, source_target_pairs={{0,64},{32,96},{64,0},{96,32},{128,192},{160,224},{192,128},{224,1... | collective-permute-start | bytes 3145736 | tf_op jit(solution)/shard_map/ppermute | solution.py:32
  475.5 7.2 %collective-permute-start.40 = (bf16[4,1,64,256]{3,2,0,1:T(8,128)(2,1)S(1)}, bf16[4,1,64,256]{3,2,0,1:T(8,128)(2,1)S(1)}, u32[]{:S(2)}, u32[]{:S(2)}) collective-permute-start(bf16[4,1,64,256]{3,2,0,1:T(8,128)(2,1)S(1)} %bitcast.278), channel_id=1, source_target_pairs={{0,4},{1,5},{2,6},{3,7},{4,0},{5,1},{6,2},{7,3},{8,12},{9,13},{10,... | collective-permute-start | bytes 393224 | tf_op jit(solution)/shard_map/ppermute | solution.py:18
  490.9 13.3 %collective-permute-start.42 = (bf16[16,1,64,256]{3,2,0,1:T(8,128)(2,1)}, bf16[16,1,64,256]{3,2,0,1:T(8,128)(2,1)}, u32[]{:S(2)}, u32[]{:S(2)}) collective-permute-start(bf16[16,1,64,256]{3,2,0,1:T(8,128)(2,1)} %bitcast.151), channel_id=1, source_target_pairs={{0,16},{1,17},{2,18},{3,19},{4,20},{5,21},{6,22},{7,23},{8,24},{9,... | collective-permute-start | bytes 1572872 | tf_op jit(solution)/shard_map/ppermute | solution.py:18
  506.8 22.1 %collective-permute-start.43 = (bf16[1,2048,256]{2,1,0:T(8,128)(2,1)}, bf16[1,2048,256]{2,1,0:T(8,128)(2,1)}, u32[]{:S(2)}, u32[]{:S(2)}) collective-permute-start(bf16[1,2048,256]{2,1,0:T(8,128)(2,1)} %bitcast.153), channel_id=1, source_target_pairs={{0,32},{32,0},{64,96},{96,64},{128,160},{160,128},{192,224},{224,1... | collective-permute-start | bytes 3145736 | tf_op jit(solution)/shard_map/ppermute | solution.py:32
  (34 other events, 861.4 us)
